TPU v7x, 32 devices: a whole 2x2x4 slice. The times are simulated.
32 devices in a mesh: dp: 8 (over y, x, core), mp: 4 (over z).
Axes of the slice: x: 2, y: 2, z: 4, core: 2. Of those that a mesh axis runs over, the one named last changes fastest.
Arguments:
- tokens: bfloat16 [31360, 768], P(('dp', 'mp')), may hold values from -36 to 36
- cotangent: bfloat16 [31360, 768], P(('dp', 'mp')), may hold values from -5 to 5
- slot_live: int32 [8, 11], P('dp'), may hold values from 0 to 1, as said below
- vectors: float32 [6, 768], replicated, may hold values from -1.2 to 1.6, as said below
- vectors_momentum: float32 [6, 768], replicated, may hold values from -512 to 512
- vectors_average: float32 [6, 768], replicated, may hold values from -1.2 to 1.6, as said below
- column_bias: float32 [2, 768], P(None, 'mp'), may hold values from -1.75 to 1.75
- column_bias_momentum: float32 [2, 768], P(None, 'mp'), may hold values from -20480 to 20480
- column_bias_average: float32 [2, 768], P(None, 'mp'), may hold values from -1.75 to 1.75
- hidden_bias: float32 [3072], P('mp'), may hold values from -1.75 to 1.75
- hidden_bias_momentum: float32 [3072], P('mp'), may hold values from -320 to 320
- hidden_bias_average: float32 [3072], P('mp'), may hold values from -1.75 to 1.75
- attention_in: float32 [768, 3, 768], P('dp', None, 'mp'), may hold values from -0.21875 to 0.21875
- attention_in_momentum: float32 [768, 3, 768], P('dp', None, 'mp'), may hold values from -10240 to 10240
- attention_in_average: float32 [768, 3, 768], P('dp', None, 'mp'), may hold values from -0.21875 to 0.21875
- attention_out: float32 [768, 768], P('mp', 'dp'), may hold values from -3.5 to 3.5
- attention_out_momentum: float32 [768, 768], P('mp', 'dp'), may hold values from -56 to 56
- attention_out_average: float32 [768, 768], P('mp', 'dp'), may hold values from -3.5 to 3.5
- hidden_in: float32 [768, 3072], P('dp', 'mp'), may hold values from -0.21875 to 0.21875
- hidden_in_momentum: float32 [768, 3072], P('dp', 'mp'), may hold values from -256 to 256
- hidden_in_average: float32 [768, 3072], P('dp', 'mp'), may hold values from -0.21875 to 0.21875
- hidden_out: float32 [3072, 768], P('mp', 'dp'), may hold values from -0.109375 to 0.109375
- hidden_out_momentum: float32 [3072, 768], P('mp', 'dp'), may hold values from -512 to 512
- hidden_out_average: float32 [3072, 768], P('mp', 'dp'), may hold values from -0.109375 to 0.109375
Outputs:
- block_output: bfloat16 [31360, 768], P(('dp', 'mp'))
- input_gradient: bfloat16 [31360, 768], P(('dp', 'mp'))
- vectors_new: float32 [6, 768], replicated
- vectors_momentum_new: float32 [6, 768], replicated
- vectors_average_new: float32 [6, 768], replicated
- column_bias_new: float32 [2, 768], P(None, 'mp')
- column_bias_momentum_new: float32 [2, 768], P(None, 'mp')
- column_bias_average_new: float32 [2, 768], P(None, 'mp')
- hidden_bias_new: float32 [3072], P('mp')
- hidden_bias_momentum_new: float32 [3072], P('mp')
- hidden_bias_average_new: float32 [3072], P('mp')
- attention_in_new: float32 [768, 3, 768], P('dp', None, 'mp')
- attention_in_momentum_new: float32 [768, 3, 768], P('dp', None, 'mp')
- attention_in_average_new: float32 [768, 3, 768], P('dp', None, 'mp')
- attention_out_new: float32 [768, 768], P('mp', 'dp')
- attention_out_momentum_new: float32 [768, 768], P('mp', 'dp')
- attention_out_average_new: float32 [768, 768], P('mp', 'dp')
- hidden_in_new: float32 [768, 3072], P('dp', 'mp')
- hidden_in_momentum_new: float32 [768, 3072], P('dp', 'mp')
- hidden_in_average_new: float32 [768, 3072], P('dp', 'mp')
- hidden_out_new: float32 [3072, 768], P('mp', 'dp')
- hidden_out_momentum_new: float32 [3072, 768], P('mp', 'dp')
- hidden_out_average_new: float32 [3072, 768], P('mp', 'dp')
Inputs may be any that keep to these rules, and one draw needn't show every extreme that they name: slot_live[g, s] is 1 where slot s of data group g holds an image and 0 where it is padding; in every draw some group has all 11 slots live. `vectors`: rows 0 and 2 are positive gains. `vectors_average`: rows 0 and 2 are positive.
All inputs are finite; a program needn't handle non-finite values.
Results may differ from a plain program's by a relative error of at most 0.017.
Values may be sent and summed in bfloat16 or wider, within the bound.
A program may use at most 192 MiB of HBM per device.

v0:
```python
import math

import jax
import jax.numpy as jnp
from jax import lax
from jax.sharding import PartitionSpec as P

MODEL_WIDTH = 768
HEAD_DIM = 64
FF = 3072
PATCH_L = 784
PATCH_S = 196
SLOT_L = 3
SLOT_S = 8


EPSILON = 1e-06
MOMENTUM = 0.9
AVERAGE = 0.8
DECAY = 0.0001
SQRT_HALF = 0.7071067811865476
RATE_VECTORS = 0.06
RATE_COLUMN = 0.01
RATE_HIDDEN = 0.4
RATE_ATTENTION_IN = 0.005
RATE_ATTENTION_OUT = 0.5
RATE_HIDDEN_IN = 0.05
RATE_HIDDEN_OUT = 0.015


def layer_norm(values, gain_row, shift_row):
    centre = jnp.mean(values, axis=-1, keepdims=True)
    centred = values - centre
    spread = jnp.mean(centred * centred, axis=-1, keepdims=True)
    return centred * lax.rsqrt(spread + EPSILON) * gain_row + shift_row


def gelu_exact(values):
    return 0.5 * values * (1.0 + lax.erf(values * SQRT_HALF))


def attend_forward(queries, keys_in, values_in, factor):
    scores = (
        jnp.einsum("bqhe,bkhe->bhqk", queries, keys_in, preferred_element_type=jnp.float32) * factor
    )
    highest = jnp.max(scores, axis=-1, keepdims=True)
    weights = jnp.exp(scores - highest)
    totals = jnp.sum(weights, axis=-1, keepdims=True)
    probs_low = (weights / totals).astype(jnp.bfloat16)
    attention_result = jnp.einsum(
        "bhqk,bkhe->bqhe", probs_low, values_in, preferred_element_type=jnp.float32
    )
    return (attention_result.astype(jnp.bfloat16), (highest + jnp.log(totals))[..., 0])


def attend_backward(queries, keys_in, values_in, log_totals, grad_attended, factor):
    scores = (
        jnp.einsum("bqhe,bkhe->bhqk", queries, keys_in, preferred_element_type=jnp.float32) * factor
    )
    probs = jnp.exp(scores - log_totals[..., None])
    grad_values = jnp.einsum(
        "bhqk,bqhe->bkhe",
        probs.astype(jnp.bfloat16),
        grad_attended,
        preferred_element_type=jnp.float32,
    )
    grad_probs = jnp.einsum(
        "bqhe,bkhe->bhqk", grad_attended, values_in, preferred_element_type=jnp.float32
    )
    centre = jnp.sum(probs * grad_probs, axis=-1, keepdims=True)
    grad_scores = (probs * (grad_probs - centre)).astype(jnp.bfloat16)
    grad_queries = (
        jnp.einsum("bhqk,bkhe->bqhe", grad_scores, keys_in, preferred_element_type=jnp.float32)
        * factor
    )
    grad_keys = (
        jnp.einsum("bhqk,bqhe->bkhe", grad_scores, queries, preferred_element_type=jnp.float32)
        * factor
    )
    return (
        grad_queries.astype(jnp.bfloat16),
        grad_keys.astype(jnp.bfloat16),
        grad_values.astype(jnp.bfloat16),
    )


def split_images(stacked, heads_dev):
    boundary = SLOT_L * PATCH_L
    return (
        stacked[:boundary].reshape(SLOT_L, PATCH_L, heads_dev, HEAD_DIM),
        stacked[boundary:].reshape(SLOT_S, PATCH_S, heads_dev, HEAD_DIM),
    )


def join_images(large_part, small_part, head_columns):
    return jnp.concatenate(
        [large_part.reshape(-1, head_columns), small_part.reshape(-1, head_columns)], axis=0
    )


def nesterov(weight_old, moment_old, average_old, gradient, rate, decay):
    step_dir = gradient + decay * weight_old
    moment_new = MOMENTUM * moment_old + step_dir
    weight_new = weight_old - rate * (step_dir + MOMENTUM * moment_new)
    return (weight_new, moment_new, AVERAGE * average_old + (1.0 - AVERAGE) * weight_new)


def local(
    tokens,
    cotangent,
    slot_live,
    vectors,
    vectors_momentum,
    vectors_average,
    column_bias,
    column_bias_momentum,
    column_bias_average,
    hidden_bias,
    hidden_bias_momentum,
    hidden_bias_average,
    attention_in,
    attention_in_momentum,
    attention_in_average,
    attention_out,
    attention_out_momentum,
    attention_out_average,
    hidden_in,
    hidden_in_momentum,
    hidden_in_average,
    hidden_out,
    hidden_out_momentum,
    hidden_out_average,
):
    rows_dev = tokens.shape[0]
    rank_mp = lax.axis_index("mp")
    group_rows = rows_dev * lax.axis_size("mp")
    total_rows = group_rows * lax.axis_size("dp")
    head_columns = column_bias.shape[1]
    heads_dev = head_columns // HEAD_DIM
    units_dev = hidden_bias.shape[0]
    factor = 1.0 / math.sqrt(HEAD_DIM)
    boundary = SLOT_L * PATCH_L
    matrix_qkv, out_weight, up_weight, down_weight = (
        lax.all_gather(attention_in.astype(jnp.bfloat16), "dp", axis=0, tiled=True),
        lax.all_gather(attention_out.astype(jnp.bfloat16), "dp", axis=1, tiled=True),
        lax.all_gather(hidden_in.astype(jnp.bfloat16), "dp", axis=0, tiled=True),
        lax.all_gather(hidden_out.astype(jnp.bfloat16), "dp", axis=1, tiled=True),
    )
    matrix_flat = matrix_qkv.reshape(MODEL_WIDTH, 3 * head_columns)
    position = rank_mp * rows_dev + jnp.arange(rows_dev, dtype=jnp.int32)
    slot_index = jnp.where(
        position < boundary, position // PATCH_L, SLOT_L + (position - boundary) // PATCH_S
    )
    matches = slot_index[:, None] == jnp.arange(slot_live.shape[1], dtype=jnp.int32)[None, :]
    live_rows = jnp.sum(jnp.where(matches, slot_live, 0), axis=1).astype(jnp.float32)
    inputs = tokens.astype(jnp.float32)
    normed = layer_norm(inputs, vectors[0], vectors[1]).astype(jnp.bfloat16)
    normed_all = lax.all_gather(normed, "mp", axis=0, tiled=True)
    bias_rows = jnp.stack([column_bias[0], jnp.zeros_like(column_bias[0]), column_bias[1]]).reshape(
        -1
    )
    projected = (
        jnp.dot(normed_all, matrix_flat, preferred_element_type=jnp.float32) + bias_rows
    ).astype(jnp.bfloat16)
    heads_all = projected.reshape(group_rows, 3, heads_dev, HEAD_DIM)
    query_large, query_small = split_images(heads_all[:, 0], heads_dev)
    keys_large, keys_small = split_images(heads_all[:, 1], heads_dev)
    values_large, values_small = split_images(heads_all[:, 2], heads_dev)

    def large_forward(blocks):
        attended_one, totals_one = attend_forward(
            blocks[0][None], blocks[1][None], blocks[2][None], factor
        )
        return (attended_one[0], totals_one[0])

    out_large, totals_large = lax.map(large_forward, (query_large, keys_large, values_large))
    out_small, totals_small = attend_forward(query_small, keys_small, values_small, factor)
    attention_result = join_images(out_large, out_small, head_columns)
    row_piece = attention_result
    attn_total = lax.psum_scatter(
        jnp.dot(row_piece, out_weight, preferred_element_type=jnp.float32).astype(jnp.bfloat16),
        "mp",
        scatter_dimension=0,
        tiled=True,
    ).astype(jnp.float32)
    middle = inputs + attn_total + vectors[4]
    normed_two = layer_norm(middle, vectors[2], vectors[3]).astype(jnp.bfloat16)
    normed_two_all = lax.all_gather(normed_two, "mp", axis=0, tiled=True)
    widened_copy = (
        jnp.dot(normed_two_all, up_weight, preferred_element_type=jnp.float32) + hidden_bias
    )
    gelu_hidden = gelu_exact(widened_copy).astype(jnp.bfloat16)
    row_piece = gelu_hidden
    mlp_total = lax.psum_scatter(
        jnp.dot(row_piece, down_weight, preferred_element_type=jnp.float32).astype(jnp.bfloat16),
        "mp",
        scatter_dimension=0,
        tiled=True,
    ).astype(jnp.float32)
    block_output = (middle + mlp_total + vectors[5]).astype(jnp.bfloat16)
    grad_output = cotangent.astype(jnp.float32) * live_rows[:, None]
    grad_output_all = lax.all_gather(grad_output.astype(jnp.bfloat16), "mp", axis=0, tiled=True)
    grad_activated = jnp.dot(grad_output_all, down_weight.T, preferred_element_type=jnp.float32)
    grad_raised = jax.vjp(gelu_exact, widened_copy)[1](grad_activated)[0].astype(jnp.bfloat16)
    grad_down_full = jnp.dot(gelu_hidden.T, grad_output_all, preferred_element_type=jnp.float32)
    grad_up_full = jnp.dot(normed_two_all.T, grad_raised, preferred_element_type=jnp.float32)
    grad_hidden_bias = jnp.sum(grad_raised, axis=0, dtype=jnp.float32)
    row_piece = grad_raised
    grad_normed_two = lax.psum_scatter(
        jnp.dot(row_piece, up_weight.T, preferred_element_type=jnp.float32).astype(jnp.bfloat16),
        "mp",
        scatter_dimension=0,
        tiled=True,
    ).astype(jnp.float32)
    norm_two_pull = jax.vjp(layer_norm, middle, vectors[2], vectors[3])[1]
    grad_middle_norm, grad_gain_two, grad_shift_two = norm_two_pull(grad_normed_two)
    grad_middle = grad_output + grad_middle_norm
    grad_middle_all = lax.all_gather(grad_middle.astype(jnp.bfloat16), "mp", axis=0, tiled=True)
    grad_attended = jnp.dot(
        grad_middle_all, out_weight.T, preferred_element_type=jnp.float32
    ).astype(jnp.bfloat16)
    grad_out_full = jnp.dot(attention_result.T, grad_middle_all, preferred_element_type=jnp.float32)
    grad_att_large, grad_att_small = split_images(grad_attended, heads_dev)

    def large_backward(blocks):
        grads_one = attend_backward(
            blocks[0][None],
            blocks[1][None],
            blocks[2][None],
            blocks[3][None],
            blocks[4][None],
            factor,
        )
        return (grads_one[0][0], grads_one[1][0], grads_one[2][0])

    grad_query_large, grad_keys_large, grad_values_large = lax.map(
        large_backward, (query_large, keys_large, values_large, totals_large, grad_att_large)
    )
    grad_query_small, grad_keys_small, grad_values_small = attend_backward(
        query_small, keys_small, values_small, totals_small, grad_att_small, factor
    )
    grad_projected = jnp.stack(
        [
            join_images(grad_query_large, grad_query_small, head_columns),
            join_images(grad_keys_large, grad_keys_small, head_columns),
            join_images(grad_values_large, grad_values_small, head_columns),
        ],
        axis=1,
    ).reshape(group_rows, 3 * head_columns)
    grad_qkv_full = jnp.dot(
        normed_all.T, grad_projected, preferred_element_type=jnp.float32
    ).reshape(MODEL_WIDTH, 3, head_columns)
    column_sums = jnp.sum(grad_projected, axis=0, dtype=jnp.float32).reshape(3, head_columns)
    grad_column_bias = jnp.stack([column_sums[0], column_sums[2]])
    row_piece = grad_projected
    grad_normed = lax.psum_scatter(
        jnp.dot(row_piece, matrix_flat.T, preferred_element_type=jnp.float32).astype(jnp.bfloat16),
        "mp",
        scatter_dimension=0,
        tiled=True,
    ).astype(jnp.float32)
    norm_one_pull = jax.vjp(layer_norm, inputs, vectors[0], vectors[1])[1]
    grad_input_norm, grad_gain_one, grad_shift_one = norm_one_pull(grad_normed)
    input_gradient = (grad_middle + grad_input_norm).astype(jnp.bfloat16)
    grad_qkv_shard, grad_out_shard, grad_up_shard, grad_down_shard = (
        lax.psum_scatter(grad_qkv_full, "dp", scatter_dimension=0, tiled=True),
        lax.psum_scatter(grad_out_full, "dp", scatter_dimension=1, tiled=True),
        lax.psum_scatter(grad_up_full, "dp", scatter_dimension=0, tiled=True),
        lax.psum_scatter(grad_down_full, "dp", scatter_dimension=1, tiled=True),
    )
    vector_terms = jnp.stack(
        [
            grad_gain_one,
            grad_shift_one,
            grad_gain_two,
            grad_shift_two,
            jnp.sum(grad_middle, axis=0),
            jnp.sum(grad_output, axis=0),
        ]
    )
    column_placed = lax.dynamic_update_slice(
        jnp.zeros((2, MODEL_WIDTH), jnp.float32), grad_column_bias, (0, rank_mp * head_columns)
    )
    hidden_placed = lax.dynamic_update_slice_in_dim(
        jnp.zeros((FF,), jnp.float32), grad_hidden_bias, rank_mp * units_dev, 0
    )
    vector_total, column_total, hidden_total = lax.psum(
        (vector_terms, column_placed, hidden_placed), ("dp", "mp")
    )
    column_grad = lax.dynamic_slice(column_total, (0, rank_mp * head_columns), (2, head_columns))
    hidden_grad = lax.dynamic_slice_in_dim(hidden_total, rank_mp * units_dev, units_dev, 0)
    root_rows = math.sqrt(total_rows)
    vectors_new, vectors_moment, vectors_mean = nesterov(
        vectors, vectors_momentum, vectors_average, vector_total, RATE_VECTORS / root_rows, 0.0
    )
    column_new, column_moment, column_mean = nesterov(
        column_bias,
        column_bias_momentum,
        column_bias_average,
        column_grad,
        RATE_COLUMN / root_rows,
        0.0,
    )
    hidden_new, hidden_moment, hidden_mean = nesterov(
        hidden_bias,
        hidden_bias_momentum,
        hidden_bias_average,
        hidden_grad,
        RATE_HIDDEN / root_rows,
        0.0,
    )
    qkv_new, qkv_moment, qkv_mean = nesterov(
        attention_in,
        attention_in_momentum,
        attention_in_average,
        grad_qkv_shard,
        RATE_ATTENTION_IN / root_rows,
        DECAY,
    )
    outer_new, outer_moment, outer_mean = nesterov(
        attention_out,
        attention_out_momentum,
        attention_out_average,
        grad_out_shard,
        RATE_ATTENTION_OUT / root_rows,
        DECAY,
    )
    upper_new, upper_moment, upper_mean = nesterov(
        hidden_in,
        hidden_in_momentum,
        hidden_in_average,
        grad_up_shard,
        RATE_HIDDEN_IN / root_rows,
        DECAY,
    )
    lower_new, lower_moment, lower_mean = nesterov(
        hidden_out,
        hidden_out_momentum,
        hidden_out_average,
        grad_down_shard,
        RATE_HIDDEN_OUT / root_rows,
        DECAY,
    )
    return (
        block_output,
        input_gradient,
        vectors_new,
        vectors_moment,
        vectors_mean,
        column_new,
        column_moment,
        column_mean,
        hidden_new,
        hidden_moment,
        hidden_mean,
        qkv_new,
        qkv_moment,
        qkv_mean,
        outer_new,
        outer_moment,
        outer_mean,
        upper_new,
        upper_moment,
        upper_mean,
        lower_new,
        lower_moment,
        lower_mean,
    )


def solution(mesh):
    placed = (
        P(("dp", "mp"), None),
        P(("dp", "mp"), None),
        P("dp", None),
        P(),
        P(),
        P(),
        P(None, "mp"),
        P(None, "mp"),
        P(None, "mp"),
        P("mp"),
        P("mp"),
        P("mp"),
        P("dp", None, "mp"),
        P("dp", None, "mp"),
        P("dp", None, "mp"),
        P("mp", "dp"),
        P("mp", "dp"),
        P("mp", "dp"),
        P("dp", "mp"),
        P("dp", "mp"),
        P("dp", "mp"),
        P("mp", "dp"),
        P("mp", "dp"),
        P("mp", "dp"),
    )
    return jax.shard_map(
        local,
        mesh=mesh,
        in_specs=placed,
        out_specs=(
            P(("dp", "mp"), None),
            P(("dp", "mp"), None),
            P(),
            P(),
            P(),
            P(None, "mp"),
            P(None, "mp"),
            P(None, "mp"),
            P("mp"),
            P("mp"),
            P("mp"),
            P("dp", None, "mp"),
            P("dp", None, "mp"),
            P("dp", None, "mp"),
            P("mp", "dp"),
            P("mp", "dp"),
            P("mp", "dp"),
            P("dp", "mp"),
            P("dp", "mp"),
            P("dp", "mp"),
            P("mp", "dp"),
            P("mp", "dp"),
            P("mp", "dp"),
        ),
        check_vma=False,
    )
```

profile of v0, /device:TPU:0, one launch (start us, length us, event | category | flops | bytes accessed | tf_op | source)
XLA Modules:
  0.0 1192.7 jit_solution(12104297643059579452)
XLA Ops:
  18.0 12.1 %all_gather.26 = bf16[192,768]{0,1:T(8,128)(2,1)} all-gather(bf16[192,96]{0,1:T(8,128)(2,1)S(1)} %copy.140), channel_id=1, replica_groups=mesh['dp'=8,'mp'=4] {'dp'}, dimensions={1}, use_global_device_ids=true | all-gather | bytes 331776 | tf_op jit(solution)/shard_map/all_gather | solution.py:145
  30.1 12.4 %all_gather.25 = bf16[768,3,192]{2,0,1:T(8,128)(2,1)S(1)} all-gather(bf16[96,3,192]{2,0,1:T(8,128)(2,1)S(1)} %convert_element_type.169), channel_id=1, replica_groups=mesh['dp'=8,'mp'=4] {'dp'}, dimensions={0}, use_global_device_ids=true | all-gather | bytes 995328 | tf_op jit(solution)/shard_map/all_gather | solution.py:144
  43.8 84.5 %all-gather.15.cloned.1.call-done = bf16[4,980,768]{2,1,0:T(8,128)(2,1)} async-done(((bf16[1,980,768]{2,1,0:T(8,128)(2,1)}), bf16[4,980,768]{2,1,0:T(8,128)(2,1)}) %all-gather.15.cloned.1.call-update) | async-done | bytes 6021136 | tf_op jit(solution)/shard_map/all_gather | solution.py:158
  128.3 5.0 reshape.361
  133.3 7.2 add_convert_fusion.1
  146.4 3.2 reshape.341
  150.8 2.5 reshape.345
  153.3 3.4 reshape.344
  160.3 4.0 reshape.339
  164.4 2.5 copy.131
  168.0 23.8 %while.26 = (s32[]{:T(128)}, bf16[3,784,3,64]{1,3,2,0:T(8,128)(2,1)}, f32[3,3,784]{2,1,0:T(4,128)}, bf16[3,784,3,64]{1,3,2,0:T(8,128)(2,1)}, bf16[3,784,3,64]{1,...) while((s32[]{:T(128)}, bf16[3,784,3,64]{1,3,2,0:T(8,128)(2,1)}, f32[3,3,784]{2,1,0:T(4,128)}, ...), condition=%wide.region_5.6_spmd, body=%wide.region_2.5_spmd.sunk | while | flops 488799680 | bytes 23586200 | solution.py:176
  168.1 2.3 multiply_reduce_fusion.7
  171.9 3.5 fusion.175
  179.7 3.5 fusion.175
  183.9 2.3 multiply_reduce_fusion.7
  187.6 3.6 fusion.175
  191.8 3.6 copy.134
  195.4 3.7 reshape.342
  205.6 2.8 reshape.346
  208.4 5.9 convolution_convert_fusion
  214.3 123.0 %fusion = bf16[984,768]{1,0:T(8,128)(2,1)S(1)} fusion(bf16[3920,768]{1,0:T(8,128)(2,1)} %convolution_convert_fusion), kind=kCustom, calls=%all-reduce-scatter | all-reduce-scatter fusion | flops 3022849 | bytes 7533056
  340.1 6.1 concatenate.16
  352.3 5.3 reshape.365
  357.5 13.1 %fusion.131 = f32[3920,768]{1,0:T(8,128)} fusion(bf16[3920,768]{1,0:T(8,128)(2,1)} %reshape.365, bf16[768,768]{0,1:T(8,128)(2,1)} %all-gather.13.cloned.1.call-done), kind=kOutput, calls=%fused_computation.221 | convolution fusion | flops 4624220160 | bytes 19243008 | tf_op jit(solution)/shard_map/dot_general | solution.py:203
  370.6 92.0 %all-gather.17.cloned.1.call-done = bf16[4,980,768]{2,1,0:T(8,128)(2,1)} async-done(((bf16[1,980,768]{2,1,0:T(8,128)(2,1)}), bf16[4,980,768]{2,1,0:T(8,128)(2,1)}) %all-gather.17.cloned.1.call-update) | async-done | bytes 6021136 | tf_op jit(solution)/shard_map/all_gather | solution.py:188
  462.6 5.0 reshape.363
  467.6 19.6 %all-gather.11.cloned.1.call-done = bf16[768,768]{1,0:T(8,128)(2,1)} async-done(((bf16[96,768]{1,0:T(8,128)(2,1)}), bf16[768,768]{1,0:T(8,128)(2,1)}) %all-gather.11.cloned.1.call-update) | async-done | bytes 1179664 | tf_op jit(solution)/shard_map/all_gather | solution.py:146
  487.3 14.8 %convert_reduce_fusion = (f32[768]{0:T(1024)S(1)}, bf16[3920,768]{1,0:T(8,128)(2,1)}, bf16[3920,768]{1,0:T(8,128)(2,1)S(1)}) fusion(f32[3920,768]{1,0:T(8,128)} %fusion.131, f32[768]{0:T(1024)S(1)} %copy-done.75, bf16[3920,768]{1,0:T(8,128)(2,1)} %reshape.363, bf16[768,768]{1,0:T(8,128)(2,1)} %all-gather.11.cloned.1.call-done), kind=kOutput, calls=%fused_computation.59 | convolution fusion | flops 4678409216 | bytes 31291392 | tf_op jit(solution)/shard_map/dot_general | solution.py:190
  502.1 2.6 copy-done.83
  504.7 9.0 fusion.133
  513.8 9.9 fusion.132
  523.8 10.8 convolution_convert_fusion.1
  534.6 109.6 %fusion.2 = bf16[984,768]{1,0:T(8,128)(2,1)} fusion(bf16[3920,768]{1,0:T(8,128)(2,1)} %convolution_convert_fusion.1), kind=kCustom, calls=%all-reduce-scatter.2 | all-reduce-scatter fusion | flops 3022849 | bytes 7533056
  647.7 8.3 concatenate.18
  656.1 3.3 fusion.73
  659.4 2.8 fusion.77
  662.3 2.7 fusion.126
  668.0 5.0 reshape.369
  673.4 11.4 convolution_convert_fusion.2
  691.0 87.7 %all-gather.21.cloned.1.call-done = bf16[4,980,768]{2,1,0:T(8,128)(2,1)} async-done(((bf16[1,980,768]{2,1,0:T(8,128)(2,1)}), bf16[4,980,768]{2,1,0:T(8,128)(2,1)}) %all-gather.21.cloned.1.call-update) | async-done | bytes 6021136 | tf_op jit(solution)/shard_map/all_gather | solution.py:218
  778.7 5.3 reshape.367
  784.0 6.3 convolution_bitcast_fusion
  790.3 4.7 convolution_convert_fusion.3
  796.6 4.5 fusion.99
  801.0 4.1 multiply_reduce_fusion.2
  809.9 2.5 reshape.347
  812.4 2.7 copy.143
  818.4 40.0 %while.27 = (s32[]{:T(128)}, bf16[3,784,3,64]{1,3,2,0:T(8,128)(2,1)}, bf16[3,784,3,64]{1,3,2,0:T(8,128)(2,1)}, bf16[3,784,3,64]{1,3,2,0:T(8,128)(2,1)}, bf16[3,7...) while((s32[]{:T(128)}, ...), condition=%wide.region_18.19_spmd, body=%wide.region_16.18_spmd.sunk | while | flops 1203017472 | bytes 65614412 | solution.py:236
  820.4 2.3 fusion.187
  822.7 3.2 multiply_reduce_fusion.8
  836.1 3.2 multiply_reduce_fusion.8
  847.1 2.3 fusion.187
  849.4 3.2 multiply_reduce_fusion.8
  878.8 2.5 maximum_bitcast_fusion
  883.1 7.2 bitcast_convert_fusion
  890.3 203.7 %fusion.125 = (bf16[984,768]{1,0:T(8,128)(2,1)S(1)}, bf16[984,768]{1,0:T(8,128)(2,1)S(1)}) fusion(bf16[3920,768]{1,0:T(8,128)(2,1)} %convolution_convert_fusion.2, bf16[3920,768]{1,0:T(8,128)(2,1)} %bitcast_convert_fusion), kind=kCustom, calls=%all-reduce-scatter.4 | all-reduce-scatter fusion | flops 6045697 | bytes 15065600
  1094.1 11.6 fusion.59
  1107.1 2.7 collective-permute-start.1
  1109.8 3.0 convert_reduce_fusion.1
  1113.1 6.3 concatenate.19
  1120.9 3.5 fusion.78
  1124.5 8.2 concatenate.17
  1132.7 39.8 %all-reduce.8 = (f32[6,768]{1,0:T(8,128)S(1)}, f32[2,768]{1,0:T(2,128)S(1)}, f32[3072]{0:T(1024)S(1)}) all-reduce(f32[6,768]{1,0:T(8,128)S(1)} %stack.38, f32[2,768]{1,0:T(2,128)S(1)} %dynamic_update_slice.23, f32[3072]{0:T(1024)S(1)} %copy-done.61), channel_id=1, replica_groups=mesh['dp'=8,'mp'=4] {'dp','mp'}, use_global_device_ids=true, to_apply=%region_29.30 | all-reduce | flops 9216 | bytes 73728 | tf_op jit(solution)/shard_map/psum | solution.py:287
  1174.5 6.4 add_convert_fusion.2
  (324 shorter events, 127.1 us)
Async XLA Ops:
  7.2 5.2 copy-start
  7.2 121.1 %all-gather.15.cloned.1.call-start = ((), (), s32[]{:S(2)}) async-start(), calls=%async_computation.9 | async-start | bytes 7557120 | tf_op jit(solution)/shard_map/all_gather | solution.py:158
  9.0 5.1 copy-start.51
  9.0 5.2 copy-start.81
  9.1 5.3 copy-start.22
  12.4 649.9 %copy-start.49 = (f32[768]{0:T(1024)}, f32[768]{0:T(1024)S(1)}, u32[]{:S(2)}) copy-start(f32[768]{0:T(1024)S(1)} %get-tuple-element.173) | copy-start | bytes 9220
  14.2 338.1 %all-gather.19.cloned.1.call-start = ((), (), s32[]{:S(2)}) async-start(), calls=%async_computation.11 | async-start | bytes 7557120 | tf_op jit(solution)/shard_map/all_gather | solution.py:202
  14.4 15.7 %copy-start.63 = (f32[980]{0:T(1024)}, f32[980]{0:T(1024)S(1)}, u32[]{:S(2)}) copy-start(f32[980]{0:T(1024)S(1)} %convert_element_type.185) | copy-start | bytes 11764
  15.8 341.7 %all-gather.13.cloned.1.call-start = ((), (), s32[]{:S(2)}) async-start(), calls=%async_computation.5 | async-start | bytes 1327104 | tf_op jit(solution)/shard_map/all_gather | solution.py:147
  16.6 446.0 %all-gather.17.cloned.1.call-start = ((), (), s32[]{:S(2)}) async-start(), calls=%async_computation.10 | async-start | bytes 7557120 | tf_op jit(solution)/shard_map/all_gather | solution.py:188
  42.5 90.8 %copy-start.24 = (bf16[768,3,192]{2,0,1:T(8,128)(2,1)}, bf16[768,3,192]{2,0,1:T(8,128)(2,1)S(1)}, u32[]{:S(2)}) copy-start(bf16[768,3,192]{2,0,1:T(8,128)(2,1)S(1)} %all_gather.25) | copy-start | bytes 2654212
  150.8 5.9 copy-start.30
  153.3 45.8 %copy-start.13 = (bf16[8,196,3,64]{1,0,3,2:T(8,128)(2,1)}, bf16[8,196,3,64]{1,0,3,2:T(8,128)(2,1)S(1)}, u32[]{:S(2)}) copy-start(bf16[8,196,3,64]{1,0,3,2:T(8,128)(2,1)S(1)} %reshape.345) | copy-start | bytes 1806340
  191.8 9.5 copy-start.5
  214.3 124.3 %copy-start.82 = (u32[32]{0:T(128)S(1)}, u32[32]{0:T(128)}, u32[]{:S(2)}) copy-start(u32[32]{0:T(128)} %constant.160) | copy-start | bytes 388
  337.3 2.8 collective-permute-start
  346.2 316.1 %copy-start.3 = (bf16[996,768]{1,0:T(8,128)(2,1)}, bf16[996,768]{1,0:T(8,128)(2,1)S(1)}, u32[]{:S(2)}) copy-start(bf16[996,768]{1,0:T(8,128)(2,1)S(1)} %concatenate.16) | copy-start | bytes 4589572
  350.5 136.8 %all-gather.11.cloned.1.call-start = ((), (), s32[]{:S(2)}) async-start(), calls=%async_computation.4 | async-start | bytes 1327104 | tf_op jit(solution)/shard_map/all_gather | solution.py:146
  352.2 334.9 %reduce-scatter.19.cloned.1.call-start = ((), (), s32[]{:S(2)}) async-start(), calls=%async_computation.8 | async-start | bytes 2654208 | tf_op jit(solution)/shard_map/reduce_scatter | solution.py:269
  370.6 116.7 %copy-start.75 = (f32[768]{0:T(1024)S(1)}, f32[768]{0:T(1024)}, u32[]{:S(2)}) copy-start(f32[768]{0:T(1024)} %param.37) | copy-start | bytes 9220
  513.7 175.3 %reduce-scatter.17.cloned.1.call-start = ((), (), s32[]{:S(2)}) async-start(), calls=%async_computation.7 | async-start | bytes 2654208 | tf_op jit(solution)/shard_map/reduce_scatter | solution.py:268
  523.7 255.0 %all-gather.21.cloned.1.call-start = ((), (), s32[]{:S(2)}) async-start(), calls=%async_computation.12 | async-start | bytes 7557120 | tf_op jit(solution)/shard_map/all_gather | solution.py:218
  645.0 2.8 collective-permute-start.2
  668.0 512.9 %reduce-scatter.21.cloned.1.call-start = ((), (), s32[]{:S(2)}) async-start(), calls=%async_computation.13 | async-start | bytes 884736
  673.3 11.4 copy-start.60
  673.3 13.8 %copy-start.40 = (f32[768,96]{0,1:T(8,128)S(1)}, f32[768,96]{0,1:T(8,128)}, u32[]{:S(2)}) copy-start(f32[768,96]{0,1:T(8,128)} %param.49) | copy-start | bytes 884740
  673.3 13.8 %copy-start.45 = (f32[768,96]{0,1:T(8,128)S(1)}, f32[768,96]{0,1:T(8,128)}, u32[]{:S(2)}) copy-start(f32[768,96]{0,1:T(8,128)} %param.51) | copy-start | bytes 884740
  673.3 13.8 %copy-start.46 = (f32[768,96]{0,1:T(8,128)S(1)}, f32[768,96]{0,1:T(8,128)}, u32[]{:S(2)}) copy-start(f32[768,96]{0,1:T(8,128)} %param.50) | copy-start | bytes 884740
  673.3 15.7 %copy-start.41 = (f32[96,768]{1,0:T(8,128)S(1)}, f32[96,768]{1,0:T(8,128)}, u32[]{:S(2)}) copy-start(f32[96,768]{1,0:T(8,128)} %param.46) | copy-start | bytes 884740
  673.3 15.7 %copy-start.47 = (f32[96,768]{1,0:T(8,128)S(1)}, f32[96,768]{1,0:T(8,128)}, u32[]{:S(2)}) copy-start(f32[96,768]{1,0:T(8,128)} %param.48) | copy-start | bytes 884740
  673.4 15.7 %copy-start.48 = (f32[96,768]{1,0:T(8,128)S(1)}, f32[96,768]{1,0:T(8,128)}, u32[]{:S(2)}) copy-start(f32[96,768]{1,0:T(8,128)} %param.47) | copy-start | bytes 884740
  691.0 92.9 %copy-start.28 = (bf16[2352,192]{0,1:T(8,128)(2,1)S(1)}, bf16[2352,192]{0,1:T(8,128)(2,1)}, u32[]{:S(2)}) copy-start(bf16[2352,192]{0,1:T(8,128)(2,1)} %reshape.342) | copy-start | bytes 2709508
  691.0 93.0 %copy-start.35 = (bf16[1568,192]{0,1:T(8,128)(2,1)S(1)}, bf16[1568,192]{0,1:T(8,128)(2,1)}, u32[]{:S(2)}) copy-start(bf16[1568,192]{0,1:T(8,128)(2,1)} %reshape.346) | copy-start | bytes 1806340
  795.0 6.0 copy-start.12
  796.5 8.6 slice-start
  809.8 373.7 %reduce-scatter.15.cloned.1.call-start = ((), (), s32[]{:S(2)}) async-start(), calls=%async_computation.6 | async-start | bytes 2654208 | tf_op jit(solution)/shard_map/reduce_scatter | solution.py:266
  812.4 6.0 copy-start.6
  812.4 6.0 copy-start.7
  861.9 6.0 copy-start.26
  870.8 6.8 copy-start.36
  1094.1 11.7 copy-start.17
  1094.1 11.7 copy-start.18
  1105.8 7.3 collective-permute-start.3
  1107.1 17.4 %collective-permute-start.1 = (bf16[12,768]{1,0:T(8,128)(2,1)S(1)}, bf16[12,768]{1,0:T(8,128)(2,1)S(1)}, u32[]{:S(2)}, u32[]{:S(2)}) collective-permute-start(bf16[12,768]{1,0:T(8,128)(2,1)S(1)} %slice.104), channel_id=1, source_target_pairs={{0,1},{1,2},{2,3},{4,5},{5,6},{6,7},{8,9},{9,10},{10,11},{12,13},{... | collective-permute-start | bytes 55304
  1112.8 6.6 copy-start.1
  1112.8 6.6 copy-start.52
  1112.8 6.6 copy-start.54
  1113.1 7.6 copy-start.66
  1113.1 7.6 copy-start.59
  1120.7 11.9 copy-start.61
  1120.8 51.7 %copy-start.74 = (f32[2,192]{1,0:T(2,128)S(1)}, f32[2,192]{1,0:T(2,128)}, u32[]{:S(2)}) copy-start(f32[2,192]{1,0:T(2,128)} %param.34) | copy-start | bytes 4612
  1120.8 51.7 %copy-start.79 = (f32[2,192]{1,0:T(2,128)S(1)}, f32[2,192]{1,0:T(2,128)}, u32[]{:S(2)}) copy-start(f32[2,192]{1,0:T(2,128)} %param.36) | copy-start | bytes 4612
  1120.8 51.7 %copy-start.80 = (f32[2,192]{1,0:T(2,128)S(1)}, f32[2,192]{1,0:T(2,128)}, u32[]{:S(2)}) copy-start(f32[2,192]{1,0:T(2,128)} %param.35) | copy-start | bytes 4612
  1120.8 52.3 %copy-start.76 = (f32[768]{0:T(1024)S(1)}, f32[768]{0:T(1024)}, u32[]{:S(2)}) copy-start(f32[768]{0:T(1024)} %param.37) | copy-start | bytes 9220
  1120.8 52.3 %copy-start.77 = (f32[768]{0:T(1024)S(1)}, f32[768]{0:T(1024)}, u32[]{:S(2)}) copy-start(f32[768]{0:T(1024)} %param.39) | copy-start | bytes 9220
  1120.8 52.3 %copy-start.78 = (f32[768]{0:T(1024)S(1)}, f32[768]{0:T(1024)}, u32[]{:S(2)}) copy-start(f32[768]{0:T(1024)} %param.38) | copy-start | bytes 9220
  1120.8 53.0 %copy-start.57 = (f32[6,768]{1,0:T(8,128)S(1)}, f32[6,768]{1,0:T(8,128)}, u32[]{:S(2)}) copy-start(f32[6,768]{1,0:T(8,128)} %param.31) | copy-start | bytes 55300
  1120.8 53.0 %copy-start.67 = (f32[6,768]{1,0:T(8,128)S(1)}, f32[6,768]{1,0:T(8,128)}, u32[]{:S(2)}) copy-start(f32[6,768]{1,0:T(8,128)} %param.33) | copy-start | bytes 55300
  1120.9 53.0 %copy-start.68 = (f32[6,768]{1,0:T(8,128)S(1)}, f32[6,768]{1,0:T(8,128)}, u32[]{:S(2)}) copy-start(f32[6,768]{1,0:T(8,128)} %param.32) | copy-start | bytes 55300
  1120.9 53.6 %copy-start.4 = (bf16[996,768]{1,0:T(8,128)(2,1)S(1)}, bf16[996,768]{1,0:T(8,128)(2,1)}, u32[]{:S(2)}) copy-start(bf16[996,768]{1,0:T(8,128)(2,1)} %copy-done.3) | copy-start | bytes 4589572
  1120.9 53.6 %copy-start.50 = (f32[768]{0:T(1024)S(1)}, f32[768]{0:T(1024)}, u32[]{:S(2)}) copy-start(f32[768]{0:T(1024)} %copy-done.49) | copy-start | bytes 9220
  1174.5 7.4 copy-start.44
  1174.5 7.4 copy-start.55
  1174.5 9.0 copy-start.42
  (39 other events, 107.6 us)
Sparse Core Ops, SparseCore 0:
  14.3 113.9 all-gather.14
  130.5 131.7 all-gather.18
  264.7 21.8 all-gather.12
  350.6 111.9 all-gather.16
  464.9 22.3 all-gather.10
  513.8 42.4 reduce-scatter.18
  560.1 42.4 reduce-scatter.16
  668.1 110.5 all-gather.20
  809.9 33.2 reduce-scatter.20
  1113.0 41.1 reduce-scatter.14
where the time goes:
time: 1200 us; the launch traced here: 1190 us
  blocking collectives  500 us (42%)
  waiting for transfers between devices  286 us (24%)
  matrix products  176 us (15%)
  local copies, waits for them, and re-layouts  141 us (12%)
  other arithmetic  66.2 us (6%)
  between operations  16.4 us (1%)
    unnamed x3, blocking collectives  436 us
    all_gather x1, waiting for transfers between devices, local(): normed_two_all = lax.all_gather(normed_two, 'mp', axis=0, tiled=True)  92 us
    all_gather x1, waiting for transfers between devices, local(): lax.all_gather(grad_middle.astype(jnp.bfloat16), 'mp', axis=0, tiled=True)  87.7 us
    all_gather x1, waiting for transfers between devices, local(): normed_all = lax.all_gather(normed, 'mp', axis=0, tiled=True)  84.5 us
    unnamed x186, local copies, waits for them, and re-layouts  65.5 us
    psum x1, blocking collectives, local(): lax.psum((vector_terms, column_placed, hidden_placed), ('dp', 'mp'))  39.8 us
  transfers between devices with their start and end apart: 14, of which 6 were waited for; matrix products, arithmetic and copies ran while one was open for 63% of the time, Pallas kernels for 0%

commit v1 on v0

v1 whole, which is shorter than its diff:
```python
import functools
import math

import jax
import jax.numpy as jnp
from jax import lax
from jax.experimental import pallas as pl
from jax.experimental.pallas import tpu as pltpu
from jax.sharding import PartitionSpec as P

F32, BF16 = jnp.float32, jnp.bfloat16
WIDTH = 768
HEAD_DIM = 64
PATCH_L = 784
PATCH_S = 196
SLOT_L = 3
SLOT_S = 8
UNIT = 196
ROWS = 208
UNITS = 8
BLOCK = 4 * ROWS
PAIRS = 6
CHUNKS = 3
COLS = 2304

EPSILON = 1e-06
MOMENTUM = 0.9
AVERAGE = 0.8
DECAY = 0.0001
RATE_VECTORS = 0.06
RATE_COLUMN = 0.01
RATE_HIDDEN = 0.4
RATE_ATTENTION_IN = 0.005
RATE_ATTENTION_OUT = 0.5
RATE_HIDDEN_IN = 0.05
RATE_HIDDEN_OUT = 0.015


def nn(a, b):
    return lax.dot_general(a, b, (((1,), (0,)), ((), ())), preferred_element_type=F32)


def nt(a, b):
    return lax.dot_general(a, b, (((1,), (1,)), ((), ())), preferred_element_type=F32)


def tn(a, b):
    return lax.dot_general(a, b, (((0,), (0,)), ((), ())), preferred_element_type=F32)


def normalize(values):
    centred = values - jnp.mean(values, axis=-1, keepdims=True)
    spread = jnp.mean(centred * centred, axis=-1, keepdims=True)
    scale = lax.rsqrt(spread + EPSILON)
    return centred * scale, scale


def norm_back(cotangent, gain, n, scale):
    cg = cotangent * gain
    return scale * (
        cg - jnp.mean(cg, axis=-1, keepdims=True) - n * jnp.mean(cg * n, axis=-1, keepdims=True)
    )


def column_sums(values):
    return jnp.sum(values, axis=0, keepdims=True)


def split_three(column):
    high = column.astype(BF16)
    rest = column - high.astype(F32)
    mid = rest.astype(BF16)
    low = (rest - mid.astype(F32)).astype(BF16)
    return high, mid, low


def gelu_terms(u):
    e = jnp.exp(u * u * -0.5)
    k = 1.0 / (1.0 + jnp.abs(u) * (0.3275911 * math.sqrt(0.5)))
    poly = k * (
        0.5 * 0.254829592
        + k * (0.5 * -0.284496736 + k * (0.5 * 1.421413741 + k * (0.5 * -1.453152027 + k * (0.5 * 1.061405429))))
    )
    tail = poly * e
    big_phi = jnp.where(u < 0.0, tail, 1.0 - tail)
    return big_phi, u * e * (1.0 / math.sqrt(2.0 * math.pi))


def block_of(ref, b):
    return ref[pl.ds(4 * b, 4)].reshape(BLOCK, ref.shape[-1])


def put_block(ref, b, value):
    ref[pl.ds(4 * b, 4)] = value.reshape(4, ROWS, value.shape[-1])


def lanes():
    return lax.broadcasted_iota(jnp.int32, (1, 128), 1)


def pad_bias(rows):
    at = lax.broadcasted_iota(jnp.int32, (rows, 1), 0)
    return jnp.where(lax.rem(at, ROWS) >= UNIT, -1e30, 0.0).astype(F32)


def masks(h):
    lane = lanes()
    own = (lane < 64) if h == 0 else (lane >= 64)
    first = 64 if h == 0 else 0
    return lane, own, first


def extend_keys(k, h, pad):
    lane, own, first = masks(h)
    ext = jnp.where(lane == first, pad, jnp.where((lane > first) & (lane < first + 4), 1.0, 0.0))
    return jnp.where(own, k.astype(F32), ext).astype(BF16)


def extend_queries(q, h, column=None):
    lane, own, first = masks(h)
    ext = jnp.where(lane == first, 1.0, 0.0).astype(F32)
    if column is not None:
        for i, part in enumerate(split_three(-column)):
            ext = jnp.where(lane == first + 1 + i, part.astype(F32), ext)
    return jnp.where(own, q.astype(F32), ext).astype(BF16)


def extend_grads(g, h, column):
    lane, own, first = masks(h)
    ext = jnp.zeros((1, 128), F32)
    for i, part in enumerate(split_three(-column)):
        ext = jnp.where(lane == first + 1 + i, part.astype(F32), ext)
    return jnp.where(own, g.astype(F32), ext).astype(BF16)


def extend_values(v, h):
    lane, own, first = masks(h)
    ext = jnp.where((lane > first) & (lane < first + 4), 1.0, 0.0)
    return jnp.where(own, v.astype(F32), ext).astype(BF16)


def attend_pair(q, k, v, pad):
    outs, logs = [], []
    for h in (0, 1):
        s = nt(extend_queries(q, h), extend_keys(k, h, pad))
        top = jnp.max(s, axis=-1, keepdims=True)
        e = jnp.exp(s - top)
        total = jnp.sum(e, axis=-1, keepdims=True)
        outs.append(nn(e.astype(BF16), v) * (1.0 / total))
        logs.append(top + jnp.log(total))
    return jnp.where(lanes() < 64, outs[0], outs[1]).astype(BF16), logs


def attend_pair_back(q, k, v, g, logs, dots, pad):
    dq, dk, dv = [], [], []
    for h in (0, 1):
        p = jnp.exp(nt(extend_queries(q, h, logs[h]), extend_keys(k, h, pad)))
        dp = nt(extend_grads(g, h, dots[h]), extend_values(v, h))
        ds = (p * dp).astype(BF16)
        dv.append(tn(p.astype(BF16), g))
        dq.append(nn(ds, k))
        dk.append(tn(ds, q))
    left = lanes() < 64
    return [jnp.where(left, t[0], t[1]).astype(BF16) for t in (dq, dk, dv)]


def lane_column(values, lane):
    return jnp.sum(jnp.where(lanes() == lane, values, 0.0), axis=-1, keepdims=True)


def kernel(
    x_ref, dy_in, g_in, vec_ref, qb_ref, hb_ref,
    yout, gin, gout, small_ref, six_ref,
    g, wb, qkv, att, h2, dy, y, e, lse, zdu, sem,
):
    rank = lax.axis_index("mp")
    large = rank < 3
    blocks = jnp.where(large, 1, 2)
    vrow = lambda i: vec_ref[i : i + 1, :]

    copies = [pltpu.make_async_copy(g_in, g, sem.at[0]), pltpu.make_async_copy(dy_in, dy, sem.at[1])]
    for c in copies:
        c.start()
    for c in copies:
        c.wait()
    small_ref[...] = jnp.zeros_like(small_ref)
    six_ref[...] = jnp.zeros_like(six_ref)

    def unpack_b():
        parts = [g[z, :, 384:768] for z in range(4)]
        o01 = [t[:, 0:128] for t in parts]
        qs, ks, vs, o2 = ([t[:, 128 + 64 * i : 192 + 64 * i] for t in parts] for i in range(4))
        cat = lambda a, b: jnp.concatenate([a, b], axis=1)
        cols = []
        for i in (0, 2):
            cols += [cat(qs[i], qs[i + 1]), cat(ks[i], ks[i + 1]), cat(vs[i], vs[i + 1])]
        cols += o01 + [cat(o2[0], o2[1]), cat(o2[2], o2[3])]
        for i, t in enumerate(cols):
            wb[:, 128 * i : 128 * (i + 1)] = t

    unpack_b()

    def w_pair(i):
        if i < 2:
            return jnp.concatenate([g[2 * i, :, 0:384], g[2 * i + 1, :, 0:384]], axis=1)
        return wb[:, 0:768]

    @pl.loop(0, blocks)
    def _(b):
        n, _s = normalize(block_of(x_ref, b).astype(F32))
        h1 = (n * vrow(0) + vrow(1)).astype(BF16)
        for i in range(3):
            out = nn(h1, w_pair(i)) + qb_ref[:, 768 * i : 768 * (i + 1)]
            qkv[pl.ds(4 * b, 4), :, 768 * i : 768 * (i + 1)] = out.astype(BF16).reshape(4, ROWS, 768)

    def pair_columns(ref, u0, count, p):
        return [
            ref[pl.ds(u0, count), :, pl.ds(pl.multiple_of(384 * p + 128 * i, 128), 128)].reshape(count * ROWS, 128)
            for i in range(3)
        ]

    def forward_image(u0, count, p):
        q, k, v = pair_columns(qkv, u0, count, p)
        out, logs = attend_pair(q, k, v, pad_bias(count * ROWS))
        att[pl.ds(u0, count), :, pl.ds(pl.multiple_of(128 * p, 128), 128)] = out.reshape(count, ROWS, 128)
        old = lse[pl.ds(u0, count)].reshape(count * ROWS, 128)
        for h in (0, 1):
            old = jnp.where(lanes() == 2 * p + h, logs[h], old)
        lse[pl.ds(u0, count)] = old.reshape(count, ROWS, 128)

    @pl.when(large)
    def _():
        pl.loop(0, PAIRS)(lambda p: forward_image(0, 4, p))

    @pl.when(jnp.logical_not(large))
    def _():
        @pl.loop(0, UNITS)
        def _(u):
            for p in range(PAIRS):
                forward_image(u, 1, p)

    def middle_of(b):
        return block_of(x_ref, b).astype(F32) + nt(block_of(att, b), wb[:, 768:1536]) + vrow(4)

    @pl.loop(0, blocks)
    def _(b):
        mid = middle_of(b)
        n, _s = normalize(mid)
        put_block(h2, b, (n * vrow(2) + vrow(3)).astype(BF16))
        put_block(y, b, mid + vrow(5))
        put_block(e, b, jnp.zeros((BLOCK, WIDTH), F32))

    @pl.loop(0, 2 * CHUNKS)
    def _(s):
        c, zp = s // 2, s % 2
        at = pl.multiple_of(768 + 512 * c, 128)
        up = jnp.concatenate([g[2 * zp, :, pl.ds(at, 256)], g[2 * zp + 1, :, pl.ds(at, 256)]], axis=1)
        at2 = pl.multiple_of(at + 256, 128)
        down = jnp.concatenate([g[2 * zp, :, pl.ds(at2, 256)], g[2 * zp + 1, :, pl.ds(at2, 256)]], axis=1)
        hb = hb_ref[pl.ds(s, 1), :]

        @pl.loop(0, blocks)
        def _(b):
            u = nn(block_of(h2, b), up) + hb
            dz = nn(block_of(dy, b), down)
            big_phi, small_phi = gelu_terms(u)
            z = (u * big_phi).astype(BF16)
            du = (dz * (big_phi + small_phi)).astype(BF16)
            zdu[pl.ds(4 * b, 4), :, 0:512] = z.reshape(4, ROWS, 512)
            zdu[pl.ds(4 * b, 4), :, 512:1024] = du.reshape(4, ROWS, 512)
            six_ref[s, 0:1, :] += column_sums(du.astype(F32))
            put_block(y, b, block_of(y, b) + nt(z, down))
            put_block(e, b, block_of(e, b) + nt(du, up))

        def grads(count):
            rows = count * ROWS
            h2v, dyv = h2[0:count].reshape(rows, WIDTH), dy[0:count].reshape(rows, WIDTH)
            gu = tn(h2v, zdu[0:count, :, 512:1024].reshape(rows, 512)).astype(BF16)
            gd = tn(dyv, zdu[0:count, :, 0:512].reshape(rows, 512)).astype(BF16)
            for i in range(2):
                g[2 * zp + i, :, pl.ds(at, 256)] = gu[:, 256 * i : 256 * (i + 1)]
                g[2 * zp + i, :, pl.ds(at2, 256)] = gd[:, 256 * i : 256 * (i + 1)]

        pl.when(large)(lambda: grads(4))
        pl.when(jnp.logical_not(large))(lambda: grads(8))

    @pl.loop(0, blocks)
    def _(b):
        zdu[pl.ds(4 * b, 4), :, 0:768] = block_of(y, b).astype(BF16).reshape(4, ROWS, WIDTH)
        n, scale = normalize(middle_of(b))
        grad = block_of(e, b)
        dyv = block_of(dy, b).astype(F32)
        dmid = dyv + norm_back(grad, vrow(2), n, scale)
        small_ref[2:3, :] += column_sums(grad * n)
        small_ref[3:4, :] += column_sums(grad)
        small_ref[4:5, :] += column_sums(dmid)
        small_ref[5:6, :] += column_sums(dyv)
        put_block(e, b, dmid)
        put_block(h2, b, dmid.astype(BF16))

    out_copy = pltpu.make_async_copy(zdu.at[:, :, 0:768], yout, sem.at[0])
    out_copy.start()

    def out_grads(count):
        rows = count * ROWS
        go = tn(h2[0:count].reshape(rows, WIDTH), att[0:count].reshape(rows, WIDTH)).astype(BF16)
        for z in range(4):
            g[z, :, 384:512] = go[:, 128 * z : 128 * (z + 1)]
            g[z, :, 704:768] = go[:, 512 + 64 * z : 576 + 64 * z]

    pl.when(large)(lambda: out_grads(4))
    pl.when(jnp.logical_not(large))(lambda: out_grads(8))

    @pl.loop(0, blocks)
    def _(b):
        put_block(dy, b, nn(block_of(h2, b), wb[:, 768:1536]).astype(BF16))

    def backward_image(u0, count, p):
        rows = count * ROWS
        q, k, v = pair_columns(qkv, u0, count, p)
        at = pl.multiple_of(128 * p, 128)
        grad = dy[pl.ds(u0, count), :, pl.ds(at, 128)].reshape(rows, 128)
        out = att[pl.ds(u0, count), :, pl.ds(at, 128)].reshape(rows, 128)
        prod = grad.astype(F32) * out.astype(F32)
        left = lanes() < 64
        dots = [
            jnp.sum(jnp.where(left, prod, 0.0), axis=-1, keepdims=True),
            jnp.sum(jnp.where(left, 0.0, prod), axis=-1, keepdims=True),
        ]
        all_logs = lse[pl.ds(u0, count)].reshape(rows, 128)
        logs = [lane_column(all_logs, 2 * p + h) for h in (0, 1)]
        parts = attend_pair_back(q, k, v, grad, logs, dots, pad_bias(rows))
        for i, part in enumerate(parts):
            qkv[pl.ds(u0, count), :, pl.ds(pl.multiple_of(384 * p + 128 * i, 128), 128)] = part.reshape(count, ROWS, 128)
        six_ref[p, 1:2, 0:128] += column_sums(parts[0].astype(F32))
        six_ref[p, 1:2, 128:256] += column_sums(parts[2].astype(F32))

    @pl.when(large)
    def _():
        pl.loop(0, PAIRS)(lambda p: backward_image(0, 4, p))

    @pl.when(jnp.logical_not(large))
    def _():
        @pl.loop(0, UNITS)
        def _(u):
            for p in range(PAIRS):
                backward_image(u, 1, p)

    out_copy.wait()

    @pl.loop(0, blocks)
    def _(b):
        n, scale = normalize(block_of(x_ref, b).astype(F32))
        put_block(h2, b, (n * vrow(0) + vrow(1)).astype(BF16))
        grad = nt(block_of(qkv, b)[:, 0:768], w_pair(0))
        grad += nt(block_of(qkv, b)[:, 768:1536], w_pair(1))
        grad += nt(block_of(qkv, b)[:, 1536:2304], w_pair(2))
        small_ref[0:1, :] += column_sums(grad * n)
        small_ref[1:2, :] += column_sums(grad)
        out = block_of(e, b) + norm_back(grad, vrow(0), n, scale)
        zdu[pl.ds(4 * b, 4), :, 0:768] = out.astype(BF16).reshape(4, ROWS, WIDTH)

    in_copy = pltpu.make_async_copy(zdu.at[:, :, 0:768], gin, sem.at[0])
    in_copy.start()

    def in_grads(count):
        rows = count * ROWS
        h1 = h2[0:count].reshape(rows, WIDTH)
        for i in range(3):
            gq = tn(h1, qkv[0:count, :, 768 * i : 768 * (i + 1)].reshape(rows, 768)).astype(BF16)
            if i < 2:
                g[2 * i, :, 0:384] = gq[:, 0:384]
                g[2 * i + 1, :, 0:384] = gq[:, 384:768]
            else:
                for z in range(4):
                    base = 384 * (z // 2) + 64 * (z % 2)
                    for t in range(3):
                        g[z, :, 512 + 64 * t : 576 + 64 * t] = gq[:, base + 128 * t : base + 128 * t + 64]

    pl.when(large)(lambda: in_grads(4))
    pl.when(jnp.logical_not(large))(lambda: in_grads(8))

    g_copy = pltpu.make_async_copy(g, gout, sem.at[1])
    g_copy.start()
    in_copy.wait()
    g_copy.wait()


def run_kernel(x, dy, weights, vectors, qkv_bias, hidden_rows):
    vmem, hbm = pl.BlockSpec(memory_space=pltpu.VMEM), pl.BlockSpec(memory_space=pl.ANY)
    units = (UNITS, ROWS, WIDTH)
    return pl.pallas_call(
        kernel,
        out_shape=[
            jax.ShapeDtypeStruct(units, BF16),
            jax.ShapeDtypeStruct(units, BF16),
            jax.ShapeDtypeStruct((4, WIDTH, COLS), BF16),
            jax.ShapeDtypeStruct((8, 768), F32),
            jax.ShapeDtypeStruct((6, 8, 512), F32),
        ],
        in_specs=[vmem, hbm, hbm, vmem, vmem, vmem],
        out_specs=[hbm, hbm, hbm, vmem, vmem],
        scratch_shapes=[
            pltpu.VMEM((4, WIDTH, COLS), BF16),
            pltpu.VMEM((WIDTH, 1536), BF16),
            pltpu.VMEM((UNITS, ROWS, COLS), BF16),
            pltpu.VMEM(units, BF16),
            pltpu.VMEM(units, BF16),
            pltpu.VMEM(units, BF16),
            pltpu.VMEM(units, F32),
            pltpu.VMEM(units, F32),
            pltpu.VMEM((UNITS, ROWS, 128), F32),
            pltpu.VMEM((UNITS, ROWS, 1024), BF16),
            pltpu.SemaphoreType.DMA((2,)),
        ],
        compiler_params=pltpu.CompilerParams(vmem_limit_bytes=64 * 2**20 - 2**16),
    )(x, dy, weights, vectors, qkv_bias, hidden_rows)


def pack_shard(attention_in, attention_out, hidden_in, hidden_out):
    q, k, v = attention_in[:, 0] * 0.125, attention_in[:, 1], attention_in[:, 2]
    out_t, down_t = attention_out.T, hidden_out.T
    cols = [q[:, :128], k[:, :128], v[:, :128], out_t[:, :128], q[:, 128:], k[:, 128:], v[:, 128:], out_t[:, 128:]]
    for c in range(CHUNKS):
        cols += [hidden_in[:, 256 * c : 256 * (c + 1)], down_t[:, 256 * c : 256 * (c + 1)]]
    return jnp.concatenate([t.astype(BF16) for t in cols], axis=1)


def unpack_shard(grad):
    q = jnp.concatenate([grad[:, 0:128], grad[:, 512:576]], axis=1) * 0.125
    k = jnp.concatenate([grad[:, 128:256], grad[:, 576:640]], axis=1)
    v = jnp.concatenate([grad[:, 256:384], grad[:, 640:704]], axis=1)
    out_t = jnp.concatenate([grad[:, 384:512], grad[:, 704:768]], axis=1)
    up = jnp.concatenate([grad[:, 768 + 512 * c : 1024 + 512 * c] for c in range(CHUNKS)], axis=1)
    down = jnp.concatenate([grad[:, 1024 + 512 * c : 1280 + 512 * c] for c in range(CHUNKS)], axis=1)
    return jnp.stack([q, k, v], axis=1), out_t.T, up, down.T


def nesterov(weight_old, moment_old, average_old, gradient, rate, decay):
    step_dir = gradient + decay * weight_old
    moment_new = MOMENTUM * moment_old + step_dir
    weight_new = weight_old - rate * (step_dir + MOMENTUM * moment_new)
    return (weight_new, moment_new, AVERAGE * average_old + (1.0 - AVERAGE) * weight_new)


def pair_order(blocks):
    first = [blocks[z, 0:2].reshape(128) for z in range(4)]
    return first + [blocks[0:2, 2].reshape(128), blocks[2:4, 2].reshape(128)]


def local(
    tokens, cotangent, slot_live,
    vectors, vectors_momentum, vectors_average,
    column_bias, column_bias_momentum, column_bias_average,
    hidden_bias, hidden_bias_momentum, hidden_bias_average,
    attention_in, attention_in_momentum, attention_in_average,
    attention_out, attention_out_momentum, attention_out_average,
    hidden_in, hidden_in_momentum, hidden_in_average,
    hidden_out, hidden_out_momentum, hidden_out_average,
):
    rows_dev = tokens.shape[0]
    rank = lax.axis_index("mp")
    total_rows = rows_dev * lax.axis_size("mp") * lax.axis_size("dp")
    own_units = rows_dev // UNIT
    unit = rank * own_units + jnp.arange(own_units, dtype=jnp.int32)
    slot = jnp.where(unit < 4 * SLOT_L, unit // 4, unit - 3 * SLOT_L)
    live = jnp.sum(
        jnp.where(slot[:, None] == jnp.arange(slot_live.shape[1], dtype=jnp.int32)[None], slot_live, 0), axis=1
    ).astype(BF16)

    def in_units(rows):
        return jnp.pad(rows.reshape(own_units, UNIT, WIDTH), ((0, 0), (0, ROWS - UNIT), (0, 0)))

    def to_work(units):
        got = lax.ppermute(units[2:5], "mp", [(0, 1), (1, 2), (2, 3)])
        row = jnp.concatenate([got, units, jnp.zeros((3, ROWS, WIDTH), BF16)], axis=0)
        return lax.dynamic_slice_in_dim(row, 3 - rank, UNITS, 0)

    def from_work(work):
        got = lax.ppermute(work[0:3], "mp", [(1, 0), (2, 1), (3, 2)])
        index = jnp.arange(own_units, dtype=jnp.int32)
        row = jnp.concatenate([work, got], axis=0)
        pick = jnp.where((rank == 3) | (index < 4 - rank), rank + index, 8 + index - (4 - rank))
        units = jnp.take(row, pick, axis=0)
        return units[:, :UNIT].reshape(rows_dev, WIDTH)

    x = to_work(in_units(tokens))
    dy = to_work(in_units(cotangent) * live[:, None, None])
    shard = pack_shard(attention_in, attention_out, hidden_in, hidden_out)
    weights = lax.all_gather(lax.all_gather(shard, "dp", axis=0, tiled=True), "mp", axis=0)
    cb = lax.all_gather(column_bias, "mp", axis=0)
    bq, bv = pair_order(cb[:, 0].reshape(4, 3, 64) * 0.125), pair_order(cb[:, 1].reshape(4, 3, 64))
    qkv_bias = jnp.concatenate([t for p in range(PAIRS) for t in (bq[p], jnp.zeros((128,), F32), bv[p])])[None]
    hb = lax.all_gather(hidden_bias, "mp", axis=0)
    hidden_rows = jnp.transpose(hb.reshape(2, 2, CHUNKS, 256), (2, 0, 1, 3)).reshape(2 * CHUNKS, 512)

    yout, gin, grads, small, six = run_kernel(x, dy, weights, vectors, qkv_bias, hidden_rows)
    block_output, input_gradient = from_work(yout), from_work(gin)
    reduced = lax.psum_scatter(grads, "mp", scatter_dimension=0, tiled=True)[0]
    reduced = lax.psum_scatter(reduced, "dp", scatter_dimension=0, tiled=True).astype(F32)
    small, six = lax.psum((small, six), ("dp", "mp"))
    vector_grad = small[0:6]
    hidden_grad = jnp.transpose(six[:, 0].reshape(CHUNKS, 2, 2, 256), (1, 2, 0, 3)).reshape(4, 768)
    hidden_grad = lax.dynamic_index_in_dim(hidden_grad, rank, 0, keepdims=False)
    pq, pv = six[:, 1, 0:128].reshape(PAIRS, 2, 64), six[:, 1, 128:256].reshape(PAIRS, 2, 64)

    def own_heads(pairs):
        second = pairs[4:6].reshape(4, 64)
        return jnp.concatenate(
            [lax.dynamic_index_in_dim(pairs, rank, 0, keepdims=False).reshape(128),
             lax.dynamic_index_in_dim(second, rank, 0, keepdims=False)]
        )

    column_grad = jnp.stack([own_heads(pq) * 0.125, own_heads(pv)])
    gqkv, gout, gup, gdown = unpack_shard(reduced)
    root = math.sqrt(total_rows)
    steps = (
        (vectors, vectors_momentum, vectors_average, vector_grad, RATE_VECTORS, 0.0),
        (column_bias, column_bias_momentum, column_bias_average, column_grad, RATE_COLUMN, 0.0),
        (hidden_bias, hidden_bias_momentum, hidden_bias_average, hidden_grad, RATE_HIDDEN, 0.0),
        (attention_in, attention_in_momentum, attention_in_average, gqkv, RATE_ATTENTION_IN, DECAY),
        (attention_out, attention_out_momentum, attention_out_average, gout, RATE_ATTENTION_OUT, DECAY),
        (hidden_in, hidden_in_momentum, hidden_in_average, gup, RATE_HIDDEN_IN, DECAY),
        (hidden_out, hidden_out_momentum, hidden_out_average, gdown, RATE_HIDDEN_OUT, DECAY),
    )
    outs = [block_output, input_gradient]
    for weight, moment, average, gradient, rate, decay in steps:
        outs.extend(nesterov(weight, moment, average, gradient, rate / root, decay))
    return tuple(outs)


def solution(mesh):
    rows, matrix, side = P(("dp", "mp"), None), P("dp", None, "mp"), P("mp", "dp")
    params = [P()] * 3 + [P(None, "mp")] * 3 + [P("mp")] * 3 + [matrix] * 3 + [side] * 3 + [P("dp", "mp")] * 3 + [side] * 3
    return jax.shard_map(
        local,
        mesh=mesh,
        in_specs=(rows, rows, P("dp", None), *params),
        out_specs=(rows, rows, *params),
        check_vma=False,
    )
```

time: 1200 us -> 933 us (0.78)
  blocking collectives: 500 us -> 199 us
  waiting for transfers between devices: 286 us -> 536 us
  matrix products: 176 us -> 0 us
  Pallas kernels: 0 us -> 113 us
  local copies, waits for them, and re-layouts: 141 us -> 30 us
  other arithmetic: 66.2 us -> 21.3 us
    unnamed x3 -> x0, blocking collectives: 436 us -> none
    reduce_scatter x3 -> x2, waiting for transfers between devices: 0.01 us -> 323 us  [the longest x1 289 us: local(): reduced = lax.psum_scatter(grads, 'mp', scatter_dimension=0, tiled=True)[0]]
    dot_general x38 -> x0, matrix products: 170 us -> none  [the longest x1 14.8 us: local(): jnp.dot(normed_two_all, up_weight, preferred_element_type=jnp.float32)]
    all_gather x6 -> x2, waiting for transfers between devices: 284 us -> 156 us  [the longest x1 119 us: local(): lax.all_gather(lax.all_gather(shard, 'dp', axis=0, tiled=True), 'mp', axi...]
    pallas_call x0 -> x1, Pallas kernels: none -> 113 us  [run_kernel(): pl.pallas_call(kernel, out_shape=[jax.ShapeDtypeStruct(units, BF16), jax....]
    all_gather x2, blocking collectives: 24.5 us -> 135 us  [the longest x1 115 us: local(): cb = lax.all_gather(column_bias, 'mp', axis=0)]
    unnamed x186 -> x86, local copies, waits for them, and re-layouts: 65.5 us -> 5.56 us
    psum x0 -> x1, waiting for transfers between devices: none -> 56.4 us  [local(): small, six = lax.psum((small, six), ('dp', 'mp'))]
  transfers between devices with their start and end apart: 14 -> 9, of which waited for: 6 -> 5; matrix products, arithmetic and copies ran while one was open for 63% -> 4% of each run, Pallas kernels for 0% -> 0%
where the time goes in v1:
time: 933 us; the launch traced here: 925 us
  waiting for transfers between devices  536 us (57%)
  blocking collectives  199 us (21%)
  Pallas kernels  113 us (12%)
  local copies, waits for them, and re-layouts  30 us (3%)
  other arithmetic  21.3 us (2%)
  between operations  15 us (2%)
  starting transfers between devices  10.5 us (1%)
    reduce_scatter x1, waiting for transfers between devices, local(): reduced = lax.psum_scatter(grads, 'mp', scatter_dimension=0, tiled=True)[0]  289 us
    all_gather x1, waiting for transfers between devices, local(): lax.all_gather(lax.all_gather(shard, 'dp', axis=0, tiled=True), 'mp', axi...  119 us
    all_gather x1, blocking collectives, local(): cb = lax.all_gather(column_bias, 'mp', axis=0)  115 us
    pallas_call x1, Pallas kernels, run_kernel(): pl.pallas_call(kernel, out_shape=[jax.ShapeDtypeStruct(units, BF16), jax....  113 us
    psum x1, blocking collectives, local(): small, six = lax.psum((small, six), ('dp', 'mp'))  63.6 us
    psum x1, waiting for transfers between devices, local(): small, six = lax.psum((small, six), ('dp', 'mp'))  56.4 us
    all_gather x1, waiting for transfers between devices, local(): lax.all_gather(shard, 'dp', axis=0, tiled=True)  36.8 us
    reduce_scatter x1, waiting for transfers between devices, local(): lax.psum_scatter(reduced, 'dp', scatter_dimension=0, tiled=True).astype(F32)  34 us
  transfers between devices with their start and end apart: 9, of which 5 were waited for; matrix products, arithmetic and copies ran while one was open for 4% of the time, Pallas kernels for 0%

profile of v1, /device:TPU:0, one launch (start us, length us, event | category | flops | bytes accessed | tf_op | source)
XLA Modules:
  0.0 924.7 jit_solution(7760986280100190391)
XLA Ops:
  7.2 1.0 copy.79
  8.3 1.0 fusion.8
  9.3 0.9 fusion.6
  10.2 1.0 convert.30
  11.2 1.0 convert_bitcast_fusion
  12.2 0.9 concatenate.64
  13.2 36.8 %all-gather.8.cloned.1.call-done = bf16[768,2304]{1,0:T(8,128)(2,1)} async-done(((bf16[96,2304]{1,0:T(8,128)(2,1)}), bf16[768,2304]{1,0:T(8,128)(2,1)}) %all-gather.8.cloned.1.call-update) | async-done | bytes 3538960 | tf_op jit(solution)/shard_map/all_gather | solution.py:490
  50.1 0.2 select_reduce_fusion
  50.3 0.3 reshape.175
  50.6 0.5 pad_multiply_fusion
  51.1 1.0 slice.250
  52.1 4.3 collective-permute-start.1
  56.5 2.3 reshape.174
  58.8 1.0 pad_slice_fusion
  59.8 3.3 collective-permute-start
  63.1 1.3 pad.7
  64.4 114.7 %all-gather.3 = f32[4,2,192]{2,1,0:T(2,128)S(1)} all-gather(f32[1,2,192]{2,1,0:T(2,128)S(1)} %bitcast.61), channel_id=3, replica_groups=mesh['dp'=8,'mp'=4] {'mp'}, dimensions={0}, use_global_device_ids=true | all-gather | bytes 7680 | tf_op jit(solution)/shard_map/all_gather | solution.py:491
  179.2 0.1 mul.266
  179.2 0.1 reshape_squeeze.49
  179.3 0.1 reshape_squeeze.50
  179.4 0.1 reshape_squeeze.51
  180.0 0.1 reshape_squeeze.58
  180.6 0.6 broadcast_in_dim.32.qb_ref
  181.2 20.7 %all-gather.4 = f32[4,1,768]{2,1,0:T(1,128)S(1)} all-gather(f32[1,1,768]{2,1,0:T(1,128)S(1)} %reshape.211), channel_id=4, replica_groups=mesh['dp'=8,'mp'=4] {'mp'}, dimensions={0}, use_global_device_ids=true | all-gather | bytes 15360 | tf_op jit(solution)/shard_map/all_gather | solution.py:494
  201.9 0.6 copy.89
  202.6 4.2 fusion.1
  206.8 118.8 %all-gather.10.cloned.1.call-done = bf16[3072,2304]{1,0:T(8,128)(2,1)} async-done(((bf16[768,2304]{1,0:T(8,128)(2,1)}), bf16[3072,2304]{1,0:T(8,128)(2,1)}) %all-gather.10.cloned.1.call-update) | async-done | bytes 14155792 | tf_op jit(solution)/shard_map/all_gather | solution.py:490
  325.5 113.4 %shard_map.407 = (bf16[8,208,768]{2,1,0:T(8,128)(2,1)}, bf16[8,208,768]{2,1,0:T(8,128)(2,1)}, bf16[4,768,2304]{2,1,0:T(8,128)(2,1)}, f32[8,768]{1,0:T(8,128)}, f32[6,8,512]{2,1,0:T(8,128)}) custom-call(bf16[8,208,768]{2,1,0:T(8,128)(2,1)} %get-tuple-element.190.x_ref, bf16[8,208,768]{2,1,0:T(8,128)(2,1)} %get-tuple-element.189.dy_in, ...), custom_call_target="tpu_custom_call" | custom-call | tf_op jit(solution)/shard_map/pallas_call | solution.py:392
  439.1 0.5 all-reduce.4.cloned.1.call-update
  439.6 288.9 %reduce-scatter.3.cloned.1.call-done = bf16[1,768,2304]{2,1,0:T(8,128)(2,1)} async-done(((bf16[4,768,2304]{2,1,0:T(8,128)(2,1)}), bf16[1,768,2304]{2,1,0:T(8,128)(2,1)}) %reduce-scatter.3.cloned.1.call-update) | async-done | bytes 3538960 | tf_op jit(solution)/shard_map/reduce_scatter | solution.py:499
  728.7 0.7 copy.83
  729.5 0.7 copy.85
  730.2 1.3 slice.222
  731.5 1.3 collective-permute-start.2
  732.8 2.2 slice.224
  735.0 1.3 collective-permute-start.3
  736.3 63.6 %psum.14 = f32[8,768]{1,0:T(8,128)S(1)} all-reduce(f32[8,768]{1,0:T(8,128)S(1)} %copy-done.18), channel_id=1, replica_groups=mesh['dp'=8,'mp'=4] {'dp','mp'}, use_global_device_ids=true, to_apply=%region_1.3 | all-reduce | flops 6144 | bytes 49152 | tf_op jit(solution)/shard_map/psum | solution.py:501
  799.9 0.6 multiply_add_fusion.8
  800.5 56.4 %all-reduce.4.cloned.1.call-done = f32[6,8,512]{2,1,0:T(8,128)} async-done(((f32[6,8,512]{2,1,0:T(8,128)}), f32[6,8,512]{2,1,0:T(8,128)}) %all-reduce.4.cloned.1.call-update) | async-done | bytes 98320 | tf_op jit(solution)/shard_map/psum | solution.py:501
  857.0 0.8 slice_reduce_fusion.3
  857.8 0.1 concatenate.68
  857.9 0.7 slice_reduce_fusion.5
  858.6 0.1 reshape.180
  858.8 0.1 reshape.181
  859.0 0.9 slice_reduce_fusion
  860.1 0.6 multiply_add_fusion.13
  860.7 0.6 multiply_add_fusion.10
  861.3 2.3 pad_maximum_fusion
  863.6 1.9 gather_fusion
  865.5 2.6 pad_maximum_fusion.1
  868.1 2.0 gather_fusion.1
  870.1 2.5 slice_select_fusion
  872.5 1.3 reshape.178
  873.9 1.3 reshape.179
  875.2 34.0 %reduce-scatter.5.cloned.1.call-done = bf16[96,2304]{1,0:T(8,128)(2,1)} async-done(((bf16[768,2304]{1,0:T(8,128)(2,1)}), bf16[96,2304]{1,0:T(8,128)(2,1)}) %reduce-scatter.5.cloned.1.call-update) | async-done | bytes 442384 | tf_op jit(solution)/shard_map/reduce_scatter | solution.py:500
  909.3 1.1 convert_element_type.12
  910.4 0.8 fusion.12
  911.2 0.9 fusion.13
  912.3 0.7 copy.86
  913.0 0.7 copy.87
  913.7 0.7 copy.88
  914.7 1.0 multiply_add_fusion
  915.7 1.0 multiply_add_fusion.2
  916.7 1.0 multiply_add_fusion.4
  (145 shorter events, 2.1 us)
Async XLA Ops:
  7.2 42.8 %all-gather.8.cloned.1.call-start = ((), (), s32[]{:S(2)}) async-start(), calls=%async_computation.2 | async-start | bytes 3981312 | tf_op jit(solution)/shard_map/all_gather | solution.py:490
  8.2 4.0 copy-start.4
  12.2 37.8 %copy-start.29 = (s32[1,11]{1,0:T(1,128)S(1)}, s32[1,11]{1,0:T(1,128)}, u32[]{:S(2)}) copy-start(s32[1,11]{1,0:T(1,128)} %param.28) | copy-start | bytes 136
  12.2 38.0 %copy-start.1 = (bf16[980,768]{1,0:T(8,128)(2,1)S(1)}, bf16[980,768]{1,0:T(8,128)(2,1)}, u32[]{:S(2)}) copy-start(bf16[980,768]{1,0:T(8,128)(2,1)} %param.27) | copy-start | bytes 4515844
  13.1 312.4 %all-gather.10.cloned.1.call-start = ((), (), s32[]{:S(2)}) async-start(), calls=%async_computation.6 | async-start | bytes 17694720 | tf_op jit(solution)/shard_map/all_gather | solution.py:490
  50.0 678.6 %reduce-scatter.3.cloned.1.call-start = ((), (), s32[]{:S(2)}) async-start(), calls=%async_computation.4 | async-start | bytes 17694720 | tf_op jit(solution)/shard_map/reduce_scatter | solution.py:499
  52.1 150.5 %collective-permute-start.1 = (bf16[3,208,768]{2,1,0:T(8,128)(2,1)}, bf16[3,208,768]{2,1,0:T(8,128)(2,1)}, u32[]{:S(2)}, u32[]{:S(2)}) collective-permute-start(bf16[3,208,768]{2,1,0:T(8,128)(2,1)} %slice.250), channel_id=1, source_target_pairs={{0,1},{1,2},{2,3},{4,5},{5,6},{6,7},{8,9},{9,10},{10,11},{12,13},{... | collective-permute-start | bytes 2875400 | tf_op jit(solution)/shard_map/ppermute | solution.py:475
  58.7 5.7 copy-start.23
  58.7 122.4 %copy-start.21 = (f32[768]{0:T(1024)S(1)}, f32[768]{0:T(1024)}, u32[]{:S(2)}) copy-start(f32[768]{0:T(1024)} %param.35) | copy-start | bytes 9220
  59.8 142.9 %collective-permute-start = (bf16[3,208,768]{2,1,0:T(8,128)(2,1)}, bf16[3,208,768]{2,1,0:T(8,128)(2,1)}, u32[]{:S(2)}, u32[]{:S(2)}) collective-permute-start(bf16[3,208,768]{2,1,0:T(8,128)(2,1)} %pad_slice_fusion), channel_id=1, source_target_pairs={{0,1},{1,2},{2,3},{4,5},{5,6},{6,7},{8,9},{9,10},{10,11},{12,13},{... | collective-permute-start | bytes 2875400 | tf_op jit(solution)/shard_map/ppermute | solution.py:475
  439.0 289.7 %copy-start.16 = (f32[192,96]{1,0:T(8,128)S(1)}, f32[192,96]{1,0:T(8,128)}, u32[]{:S(2)}) copy-start(f32[192,96]{1,0:T(8,128)} %param.42) | copy-start | bytes 221188
  439.0 290.5 %copy-start.17 = (f32[192,96]{1,0:T(8,128)S(1)}, f32[192,96]{1,0:T(8,128)}, u32[]{:S(2)}) copy-start(f32[192,96]{1,0:T(8,128)} %param.43) | copy-start | bytes 221188
  439.0 417.9 %all-reduce.4.cloned.1.call-start = ((), (), s32[]{:S(2)}) async-start(), calls=%async_computation.3 | async-start | bytes 196608 | tf_op jit(solution)/shard_map/psum | solution.py:501
  439.6 469.7 %reduce-scatter.5.cloned.1.call-start = ((), (), s32[]{:S(2)}) async-start(), calls=%async_computation.5 | async-start | bytes 3981312 | tf_op jit(solution)/shard_map/reduce_scatter | solution.py:500
  728.6 7.7 copy-start.18
  728.6 71.2 %copy-start.15 = (f32[6,768]{1,0:T(8,128)S(1)}, f32[6,768]{1,0:T(8,128)}, u32[]{:S(2)}) copy-start(f32[6,768]{1,0:T(8,128)} %vec_ref.1) | copy-start | bytes 55300
  728.6 71.2 %copy-start.19 = (f32[6,768]{1,0:T(8,128)S(1)}, f32[6,768]{1,0:T(8,128)}, u32[]{:S(2)}) copy-start(f32[6,768]{1,0:T(8,128)} %param.31) | copy-start | bytes 55300
  728.6 71.2 %copy-start.20 = (f32[6,768]{1,0:T(8,128)S(1)}, f32[6,768]{1,0:T(8,128)}, u32[]{:S(2)}) copy-start(f32[6,768]{1,0:T(8,128)} %param.30) | copy-start | bytes 55300
  728.6 131.4 %copy-start.24 = (f32[2,192]{1,0:T(2,128)S(1)}, f32[2,192]{1,0:T(2,128)}, u32[]{:S(2)}) copy-start(f32[2,192]{1,0:T(2,128)} %param.32) | copy-start | bytes 4612
  728.6 131.4 %copy-start.27 = (f32[2,192]{1,0:T(2,128)S(1)}, f32[2,192]{1,0:T(2,128)}, u32[]{:S(2)}) copy-start(f32[2,192]{1,0:T(2,128)} %param.34) | copy-start | bytes 4612
  728.7 131.4 %copy-start.28 = (f32[2,192]{1,0:T(2,128)S(1)}, f32[2,192]{1,0:T(2,128)}, u32[]{:S(2)}) copy-start(f32[2,192]{1,0:T(2,128)} %param.33) | copy-start | bytes 4612
  728.7 132.0 %copy-start.22 = (f32[768]{0:T(1024)S(1)}, f32[768]{0:T(1024)}, u32[]{:S(2)}) copy-start(f32[768]{0:T(1024)} %param.35) | copy-start | bytes 9220
  728.7 132.0 %copy-start.25 = (f32[768]{0:T(1024)S(1)}, f32[768]{0:T(1024)}, u32[]{:S(2)}) copy-start(f32[768]{0:T(1024)} %param.37) | copy-start | bytes 9220
  728.7 132.0 %copy-start.26 = (f32[768]{0:T(1024)S(1)}, f32[768]{0:T(1024)}, u32[]{:S(2)}) copy-start(f32[768]{0:T(1024)} %param.36) | copy-start | bytes 9220
  731.5 129.8 %collective-permute-start.2 = (bf16[3,208,768]{2,1,0:T(8,128)(2,1)S(1)}, bf16[3,208,768]{2,1,0:T(8,128)(2,1)}, u32[]{:S(2)}, u32[]{:S(2)}) collective-permute-start(bf16[3,208,768]{2,1,0:T(8,128)(2,1)S(1)} %slice.222), channel_id=1, source_target_pairs={{1,0},{2,1},{3,2},{5,4},{6,5},{7,6},{9,8},{10,9},{11,10},{13,12},{... | collective-permute-start | bytes 2875400 | tf_op jit(solution)/shard_map/ppermute | solution.py:480
  735.0 130.5 %collective-permute-start.3 = (bf16[3,208,768]{2,1,0:T(8,128)(2,1)}, bf16[3,208,768]{2,1,0:T(8,128)(2,1)}, u32[]{:S(2)}, u32[]{:S(2)}) collective-permute-start(bf16[3,208,768]{2,1,0:T(8,128)(2,1)} %slice.224), channel_id=1, source_target_pairs={{1,0},{2,1},{3,2},{5,4},{6,5},{7,6},{9,8},{10,9},{11,10},{13,12},{... | collective-permute-start | bytes 2875400 | tf_op jit(solution)/shard_map/ppermute | solution.py:480
  873.9 38.3 %copy-start.5 = (f32[192,96]{0,1:T(8,128)S(1)}, f32[192,96]{0,1:T(8,128)}, u32[]{:S(2)}) copy-start(f32[192,96]{0,1:T(8,128)} %copy-done.4) | copy-start | bytes 221188
  873.9 38.3 %copy-start.7 = (f32[192,96]{0,1:T(8,128)S(1)}, f32[192,96]{0,1:T(8,128)}, u32[]{:S(2)}) copy-start(f32[192,96]{0,1:T(8,128)} %copy.83) | copy-start | bytes 221188
  873.9 38.3 %copy-start.8 = (f32[192,96]{0,1:T(8,128)S(1)}, f32[192,96]{0,1:T(8,128)}, u32[]{:S(2)}) copy-start(f32[192,96]{0,1:T(8,128)} %copy.85) | copy-start | bytes 221188
  875.2 39.4 %copy-start.2 = (f32[768,96]{0,1:T(8,128)S(1)}, f32[768,96]{0,1:T(8,128)}, u32[]{:S(2)}) copy-start(f32[768,96]{0,1:T(8,128)} %param.47) | copy-start | bytes 884740
  875.2 39.4 %copy-start.9 = (f32[768,96]{0,1:T(8,128)S(1)}, f32[768,96]{0,1:T(8,128)}, u32[]{:S(2)}) copy-start(f32[768,96]{0,1:T(8,128)} %param.49) | copy-start | bytes 884740
  875.2 39.4 %copy-start.10 = (f32[768,96]{0,1:T(8,128)S(1)}, f32[768,96]{0,1:T(8,128)}, u32[]{:S(2)}) copy-start(f32[768,96]{0,1:T(8,128)} %param.48) | copy-start | bytes 884740
  909.3 5.3 copy-start
  912.2 3.5 copy-start.3
  912.2 3.5 copy-start.11
  912.2 3.5 copy-start.12
  914.5 2.1 copy-start.6
  914.6 2.1 copy-start.13
  914.6 2.1 copy-start.14
Sparse Core Ops, SparseCore 0:
  13.3 36.6 all-gather.7
  51.5 273.9 all-gather.9
  439.1 289.4 reduce-scatter.2
  734.6 122.3 all-reduce.3
  860.3 48.9 reduce-scatter.4
